TPU v7x, 32 devices: a whole 2x2x4 slice. The times are simulated.
32 devices in a mesh: groups: 2 (over y), expert: 4 (over z), replica: 4 (over x, core).
Axes of the slice: x: 2, y: 2, z: 4, core: 2. Of those that a mesh axis runs over, the one named last changes fastest.
Arguments:
- moe_rows: bfloat16 [128, 7168], P(('groups', 'expert', 'replica')), parts along dimension 0, may hold values from -6 to 6
- expert_ids: int32 [128, 8], P(('groups', 'expert', 'replica')), parts along dimension 0, may hold values from 0 to 31, all different within a row; in each aligned block of 4 rows (0 to 3, 4 to 7, ...) at most 2 rows name the same one
- expert_weights: float32 [128, 8], P(('groups', 'expert', 'replica')), parts along dimension 0, may hold values from 0.05 to 0.5
- w_gate: bfloat16 [32, 7168, 1024], P('expert', None, 'replica'), may hold values from -0.0625 to 0.0625
- w_up: bfloat16 [32, 7168, 1024], P('expert', None, 'replica'), may hold values from -0.0625 to 0.0625
- w_down: bfloat16 [32, 1024, 7168], P('expert', 'replica'), may hold values from -0.1875 to 0.1875
- queries: bfloat16 [128, 64, 576], P(('groups', 'expert', 'replica')), parts along dimension 0, may hold values from -120 to 120
- latent_cache: bfloat16 [128, 256, 576], P(('groups', 'expert', 'replica')), parts along dimension 0, may hold values from -4 to 4
- cache_lengths: int32 [128], P(('groups', 'expert', 'replica')), parts along dimension 0, may hold values from 2 to 256, as said below
- move_src: int32 [128], P(('groups', 'expert', 'replica')), parts along dimension 0, may hold values from 0 to 15, as said below
Outputs:
- moe_out: bfloat16 [128, 7168], P(('groups', 'expert', 'replica')), parts along dimension 0
- context: bfloat16 [128, 64, 512], P(('groups', 'expert', 'replica')), parts along dimension 0
There are 2 independent parts, one for each index of `groups`. A program takes and returns all parts, laid end to end along the dimension named above; an argument that names none is the same for every part. Nothing has to cross between parts.
Inputs may be any that keep to these rules, and one draw needn't show every extreme that they name: `expert_ids`: each row names 8 different experts; within the rows of one device (aligned blocks of 4 rows) no expert is named more than 2 times, a bound that some block reaches. `move_src`: each aligned block of 16 entries is a permutation of 0 to 15. `cache_lengths`: some request holds exactly 256 positions.
All inputs are finite; a program needn't handle non-finite values.
Results may differ from a plain program's by a relative error of at most 0.0057.
Values may be sent and summed in bfloat16 or wider, within the bound.
A program may use at most 256 MiB of HBM per device.

v0:
```python
import jax
import jax.numpy as jnp
from jax import lax
from jax.sharding import PartitionSpec as P

LAT = 512


score_scale = 192.0 ** (-0.5)


def attend(query_rows, cache_rows, lengths):
    scores = (
        jnp.einsum("rhc,rtc->rht", query_rows, cache_rows, preferred_element_type=jnp.float32)
        * score_scale
    )
    places = jnp.arange(cache_rows.shape[1], dtype=jnp.int32)
    visible = places[None, None, :] < lengths[:, None, None]
    scores = jnp.where(visible, scores, -jnp.inf)
    highest = jnp.max(scores, axis=2, keepdims=True)
    powers = jnp.exp(scores - highest)
    softmax_weights = (powers / jnp.sum(powers, axis=2, keepdims=True)).astype(jnp.bfloat16)
    return jnp.einsum(
        "rht,rtc->rhc", softmax_weights, cache_rows[:, :, :LAT], preferred_element_type=jnp.float32
    ).astype(jnp.bfloat16)


def slot_table(block_ids, experts, capacity):
    flat_ids = block_ids.reshape(-1)
    labels = jnp.arange(experts, dtype=jnp.int32)
    onehot = (flat_ids[:, None] == labels[None, :]).astype(jnp.int32)
    before = jnp.cumsum(onehot, axis=0) - onehot
    slot_rank = jnp.sum(before * onehot, axis=1)
    places = jnp.arange(capacity, dtype=jnp.int32)
    chosen = (flat_ids[None, None, :] == labels[:, None, None]) & (
        slot_rank[None, None, :] == places[None, :, None]
    )
    return chosen.astype(jnp.bfloat16)


def expert_block(arrived, w_gate, w_up, w_down):
    gate_out = jnp.einsum("send,edf->senf", arrived, w_gate, preferred_element_type=jnp.float32)
    up_out = jnp.einsum("send,edf->senf", arrived, w_up, preferred_element_type=jnp.float32)
    hidden = (jax.nn.silu(gate_out) * up_out).astype(jnp.bfloat16)
    return jnp.einsum("senf,efd->send", hidden, w_down, preferred_element_type=jnp.float32)


def local(
    moe_rows,
    expert_ids,
    expert_weights,
    w_gate,
    w_up,
    w_down,
    queries,
    latent_cache,
    cache_lengths,
    move_src,
):
    n_expert = lax.axis_size("expert")
    tokens, top_count = expert_ids.shape
    model_width = moe_rows.shape[1]
    local_experts = w_gate.shape[0]
    experts = local_experts * n_expert
    capacity = max(2, 3 * tokens * top_count // (2 * experts))
    routing = slot_table(expert_ids, experts, capacity)
    picked = jnp.sum(routing.reshape(experts, capacity, tokens, top_count), axis=3)
    outgoing = jnp.einsum(
        "ect,td->ecd", picked, moe_rows, preferred_element_type=jnp.float32
    ).astype(jnp.bfloat16)
    outgoing = outgoing.reshape(n_expert, local_experts, capacity, model_width)
    partials = expert_block(
        lax.all_gather(
            lax.all_to_all(outgoing, "expert", split_axis=0, concat_axis=0, tiled=True),
            "replica",
            axis=0,
            tiled=True,
        ),
        w_gate,
        w_up,
        w_down,
    )
    summed = lax.psum_scatter(partials, "replica", scatter_dimension=0, tiled=True).astype(
        jnp.bfloat16
    )
    returned = lax.all_to_all(summed, "expert", split_axis=0, concat_axis=0, tiled=True)
    results = returned.reshape(experts, capacity, model_width)
    per_route = jnp.einsum("eca,ecd->ad", routing, results, preferred_element_type=jnp.float32)
    moe_out = jnp.sum(
        per_route.reshape(tokens, top_count, model_width) * expert_weights[:, :, None], axis=1
    ).astype(jnp.bfloat16)
    requests, positions, channels = latent_cache.shape
    initial = (
        jnp.zeros((requests, positions * channels), jnp.float32),
        jnp.zeros((requests,), jnp.int32),
    )
    piece_cache = lax.all_gather(latent_cache, "replica", axis=0, tiled=True)
    piece_len = lax.all_gather(cache_lengths, "replica", axis=0, tiled=True)
    piece_rows = piece_cache.shape[0]
    chosen = move_src[:, None] == jnp.arange(piece_rows, dtype=jnp.int32)[None, :]
    moved = jnp.dot(
        chosen.astype(jnp.bfloat16),
        piece_cache.reshape(piece_rows, -1),
        preferred_element_type=jnp.float32,
    )
    lengths = jnp.sum(jnp.where(chosen, piece_len[None, :], 0), axis=1)
    moved_len = initial[1] + lengths
    context = attend(
        queries, moved.astype(jnp.bfloat16).reshape(requests, positions, channels), moved_len
    )
    return (moe_out, context)


def solution(mesh):
    return jax.shard_map(
        local,
        mesh=mesh,
        in_specs=(
            P(("groups", "expert", "replica"), None),
            P(("groups", "expert", "replica"), None),
            P(("groups", "expert", "replica"), None),
            P("expert", None, "replica"),
            P("expert", None, "replica"),
            P("expert", "replica", None),
            P(("groups", "expert", "replica"), None, None),
            P(("groups", "expert", "replica"), None, None),
            P(("groups", "expert", "replica")),
            P(("groups", "expert", "replica")),
        ),
        out_specs=(
            P(("groups", "expert", "replica"), None),
            P(("groups", "expert", "replica"), None, None),
        ),
        check_vma=False,
    )
```

profile of v0, /device:TPU:0, one launch (start us, length us, event | category | flops | bytes accessed | tf_op | source)
XLA Modules:
  0.0 270.1 jit_solution(8747979721635142555)
XLA Ops:
  7.2 0.8 eq.87
  8.0 0.8 iota_compare_fusion
  9.3 1.3 fusion.10
  10.6 0.9 copy.27
  11.5 29.0 %all_to_all.10 = bf16[4,8,2,7168]{3,2,1,0:T(2,128)(2,1)S(1)} all-to-all(bf16[4,8,2,7168]{3,2,1,0:T(2,128)(2,1)S(1)} %copy.27), channel_id=1, replica_groups=mesh['groups'=2,'expert'=4,'replica'=4] {'expert'}, dimensions={0} | all-to-all | bytes 1835008 | tf_op jit(solution)/shard_map/all_to_all | solution.py:74
  40.6 1.1 copy.28
  41.7 30.7 %all-gather.3.cloned.1.call-done = bf16[16,8,2,7168]{3,1,2,0:T(8,128)(2,1)} async-done(((bf16[4,8,2,7168]{3,1,2,0:T(8,128)(2,1)}), bf16[16,8,2,7168]{3,1,2,0:T(8,128)(2,1)}) %all-gather.3.cloned.1.call-update) | async-done | bytes 3670032 | tf_op jit(solution)/shard_map/all_gather | solution.py:73
  72.4 15.8 %fusion.19 = f32[16,8,2,256]{3,0,2,1:T(8,128)S(1)} fusion(bf16[8,7168,256]{2,1,0:T(8,128)(2,1)} %param.13, bf16[16,8,2,7168]{3,1,2,0:T(8,128)(2,1)} %all-gather.3.cloned.1.call-done), kind=kOutput, calls=%fused_computation.22 | convolution fusion | flops 939524096 | bytes 33292288 | tf_op jit(solution)/shard_map/send,edf->senf/dot_general | solution.py:42
  88.3 33.3 %fusion.7 = f32[16,8,2,7168]{3,0,2,1:T(8,128)} fusion(bf16[8,256,7168]{2,1,0:T(8,128)(2,1)} %param.15, bf16[8,7168,256]{2,1,0:T(8,128)(2,1)} %param.14, bf16[16,8,2,7168]{3,1,2,0:T(8,128)(2,1)} %all-gather.3.cloned.1.call-done, f32[16,8,2,256]{3,0,2,1:T(8,128)S(1)} %fusion.19), kind=kOutput, calls=%fused_computation.8 | convolution fusion | flops 1879441408 | bytes 69992448 | tf_op jit(solution)/shard_map/senf,efd->send/dot_general | solution.py:45
  121.6 10.3 %copy.31 = f32[16,8,2,7168]{3,1,2,0:T(8,128)} copy(f32[16,8,2,7168]{3,0,2,1:T(8,128)} %fusion.7) | data formatting | bytes 14680064 | tf_op jit(solution)/shard_map/senf,efd->send/transpose | solution.py:45
  132.0 0.7 all-gather.5.cloned.1.call-update
  134.2 4.3 %all-reduce = s32[16]{0:T(128)S(1)} all-reduce(s32[16]{0:T(128)S(1)} %dynamic-update-slice), channel_id=1, replica_groups=mesh['groups'=2,'expert'=4,'replica'=4] {'replica'}, use_global_device_ids=true, to_apply=%add | all-reduce | flops 16 | bytes 128
  138.6 58.9 %reduce-scatter.2.cloned.1.call-done = f32[4,8,2,7168]{3,1,2,0:T(8,128)} async-done(((f32[16,8,2,7168]{3,1,2,0:T(8,128)}), f32[4,8,2,7168]{3,1,2,0:T(8,128)}) %reduce-scatter.2.cloned.1.call-update) | async-done | bytes 1835024 | tf_op jit(solution)/shard_map/reduce_scatter | solution.py:83
  197.5 1.6 convert_element_type.35
  199.1 1.9 copy.32
  201.0 4.6 %all-to-all-start.1 = ((bf16[4,8,2,7168]{3,2,1,0:T(2,128)(2,1)}), bf16[4,8,2,7168]{3,2,1,0:T(2,128)(2,1)}, u32[]{:S(2)}, u32[]{:S(2)}) async-start(bf16[4,8,2,7168]{3,2,1,0:T(2,128)(2,1)} %copy.32), calls=%async_computation.2 | async-start | bytes 1835008 | tf_op jit(solution)/shard_map/all_to_all | solution.py:86
  205.8 30.8 %all-gather.5.cloned.1.call-done = bf16[16,256,576]{1,2,0:T(8,128)(2,1)} async-done(((bf16[4,256,576]{1,2,0:T(8,128)(2,1)}), bf16[16,256,576]{1,2,0:T(8,128)(2,1)}) %all-gather.5.cloned.1.call-update) | async-done | bytes 4718608 | tf_op jit(solution)/shard_map/all_gather | solution.py:97
  236.6 7.7 %copy.34 = bf16[16,256,576]{2,1,0:T(8,128)(2,1)} copy(bf16[16,256,576]{1,2,0:T(8,128)(2,1)} %all-gather.5.cloned.1.call-done) | data formatting | bytes 9437184 | tf_op jit(solution)/shard_map/all_gather | solution.py:97
  244.3 9.2 %reshape.124 = bf16[16,147456]{1,0:T(8,128)(2,1)} reshape(bf16[16,256,576]{2,1,0:T(8,128)(2,1)} %copy.34) | data formatting | bytes 9437184 | tf_op jit(solution)/shard_map/reshape | solution.py:103
  253.6 3.2 %convolution_convert_fusion = bf16[4,147456]{1,0:T(4,128)(2,1)S(1)} fusion(bf16[16,147456]{1,0:T(8,128)(2,1)} %reshape.124, s32[4]{0:T(128)S(1)} %copy-done.2), kind=kOutput, calls=%fused_computation.1 | convolution fusion | flops 19464256 | bytes 5898256 | tf_op jit(solution)/shard_map/dot_general | solution.py:101
  256.8 1.2 reshape.137
  258.0 1.1 reshape.125
  259.9 1.3 convolution_convert_fusion.2
  261.2 2.4 fusion.14
  (33 shorter events, 2.6 us)
Async XLA Ops:
  7.2 252.0 %copy-start = (bf16[4,64,576]{2,1,0:T(8,128)(2,1)S(1)}, bf16[4,64,576]{2,1,0:T(8,128)(2,1)}, u32[]{:S(2)}) copy-start(bf16[4,64,576]{2,1,0:T(8,128)(2,1)} %param.16) | copy-start | bytes 884740
  7.2 65.3 %all-gather.3.cloned.1.call-start = ((), (), s32[]{:S(2)}) async-start(), calls=%async_computation.3 | async-start | bytes 4587520 | tf_op jit(solution)/shard_map/all_gather | solution.py:73
  41.7 155.8 %reduce-scatter.2.cloned.1.call-start = ((), (), s32[]{:S(2)}) async-start(), calls=%async_computation.4 | async-start | bytes 9175040 | tf_op jit(solution)/shard_map/reduce_scatter | solution.py:83
  131.9 0.8 copy-start.5
  131.9 2.0 copy-start.4
  131.9 6.5 %copy-start.2 = (s32[4]{0:T(128)S(1)}, s32[4]{0:T(128)}, u32[]{:S(2)}) copy-start(s32[4]{0:T(128)} %param.19) | copy-start | bytes 52
  131.9 73.8 %copy-start.1 = (s32[4,8]{1,0:T(4,128)S(1)}, s32[4,8]{1,0:T(4,128)}, u32[]{:S(2)}) copy-start(s32[4,8]{1,0:T(4,128)} %param.11) | copy-start | bytes 388
  131.9 104.7 %all-gather.5.cloned.1.call-start = ((), (), s32[]{:S(2)}) async-start(), calls=%async_computation.5 | async-start | bytes 5898240 | tf_op jit(solution)/shard_map/all_gather | solution.py:97
  201.0 60.1 %all-to-all-start.1 = ((bf16[4,8,2,7168]{3,2,1,0:T(2,128)(2,1)}), bf16[4,8,2,7168]{3,2,1,0:T(2,128)(2,1)}, u32[]{:S(2)}, u32[]{:S(2)}) async-start(bf16[4,8,2,7168]{3,2,1,0:T(2,128)(2,1)} %copy.32), calls=%async_computation.2 | async-start | bytes 1835008 | tf_op jit(solution)/shard_map/all_to_all | solution.py:86
  258.0 3.2 %copy-start.3 = (f32[4,8]{1,0:T(4,128)S(1)}, f32[4,8]{1,0:T(4,128)}, u32[]{:S(2)}) copy-start(f32[4,8]{1,0:T(4,128)} %param.12) | copy-start | bytes 388
Sparse Core Ops, SparseCore 0:
  41.8 30.6 all-gather.2
  132.0 65.4 reduce-scatter.1
  199.1 37.4 all-gather.4
where the time goes:
time: 271 us; the launch traced here: 270 us
  waiting for transfers between devices  121 us (45%)
  matrix products  57.8 us (21%)
  local copies, waits for them, and re-layouts  35.2 us (13%)
  blocking collectives  33.3 us (12%)
  between operations  14.5 us (5%)
  starting transfers between devices  4.72 us (2%)
  other arithmetic  3.3 us (1%)
    reduce_scatter x1, waiting for transfers between devices, local(): lax.psum_scatter(partials, 'replica', scatter_dimension=0, tiled=True)  58.9 us
    dot_general x1, matrix products, expert_block(): jnp.einsum('senf,efd->send', hidden, w_down, preferred_element_type=jnp.f...  33.3 us
    all_gather x1, waiting for transfers between devices, local(): piece_cache = lax.all_gather(latent_cache, 'replica', axis=0, tiled=True)  30.8 us
    all_gather x1, waiting for transfers between devices, local(): lax.all_gather(lax.all_to_all(outgoing, 'expert', split_axis=0, concat_ax...  30.7 us
    all_to_all x1, blocking collectives, local(): lax.all_to_all(outgoing, 'expert', split_axis=0, concat_axis=0, tiled=True)  29 us
    dot_general x1, matrix products, expert_block(): jnp.einsum('send,edf->senf', arrived, w_gate, preferred_element_type=jnp....  15.8 us
    transpose x1, local copies, waits for them, and re-layouts, expert_block(): jnp.einsum('senf,efd->send', hidden, w_down, preferred_element_type=jnp.f...  10.3 us
    reshape x1, local copies, waits for them, and re-layouts, local(): piece_cache.reshape(piece_rows, -1)  9.25 us
  transfers between devices with their start and end apart: 4, of which 3 were waited for; matrix products, arithmetic and copies ran while one was open for 11% of the time, Pallas kernels for 0%

commit v1 on v0

v1 whole, which is shorter than its diff:
```python
import jax
import jax.numpy as jnp
from jax import lax
from jax.sharding import PartitionSpec as P

LAT = 512


score_scale = 192.0 ** (-0.5)


def attend(query_rows, cache_rows, lengths):
    scores = (
        jnp.einsum("rhc,rtc->rht", query_rows, cache_rows, preferred_element_type=jnp.float32)
        * score_scale
    )
    places = jnp.arange(cache_rows.shape[1], dtype=jnp.int32)
    visible = places[None, None, :] < lengths[:, None, None]
    scores = jnp.where(visible, scores, -jnp.inf)
    highest = jnp.max(scores, axis=2, keepdims=True)
    powers = jnp.exp(scores - highest)
    softmax_weights = (powers / jnp.sum(powers, axis=2, keepdims=True)).astype(jnp.bfloat16)
    return jnp.einsum(
        "rht,rtc->rhc", softmax_weights, cache_rows[:, :, :LAT], preferred_element_type=jnp.float32
    ).astype(jnp.bfloat16)


def pick(stack, places):
    return jnp.concatenate(
        [lax.dynamic_slice_in_dim(stack, places[i], 1, axis=0) for i in range(places.shape[0])],
        axis=0,
    )


def local(
    moe_rows,
    expert_ids,
    expert_weights,
    w_gate,
    w_up,
    w_down,
    queries,
    latent_cache,
    cache_lengths,
    move_src,
):
    n_expert = lax.axis_size("expert")
    n_dev = n_expert * lax.axis_size("replica")
    tokens = expert_ids.shape[0]
    model_width = moe_rows.shape[1]
    local_experts = w_gate.shape[0]
    experts = local_experts * n_expert
    both = ("expert", "replica")
    onehot = expert_ids[:, :, None] == jnp.arange(experts, dtype=jnp.int32)
    combine = jnp.sum(jnp.where(onehot, expert_weights[:, :, None], 0.0), axis=1)
    rows = lax.all_gather(moe_rows, both, axis=0, tiled=True)
    combine = lax.all_gather(combine, both, axis=0, tiled=True)
    mine = lax.dynamic_slice_in_dim(
        combine, lax.axis_index("expert") * local_experts, local_experts, axis=1
    )
    gate = jnp.einsum("nd,edf->enf", rows, w_gate, preferred_element_type=jnp.float32)
    up = jnp.einsum("nd,edf->enf", rows, w_up, preferred_element_type=jnp.float32)
    hidden = (jax.nn.silu(gate) * up * mine.T[:, :, None]).astype(jnp.bfloat16)
    partial = jnp.einsum("enf,efd->nd", hidden, w_down, preferred_element_type=jnp.float32)
    partial = partial.astype(jnp.bfloat16).reshape(n_dev, tokens, model_width)
    arrived = lax.all_to_all(partial, both, split_axis=0, concat_axis=0, tiled=True)
    moe_out = jnp.sum(arrived.astype(jnp.float32), axis=0).astype(jnp.bfloat16)

    requests = latent_cache.shape[0]
    all_queries = lax.all_gather(queries, "replica", axis=0, tiled=True)
    all_src = lax.all_gather(move_src, "replica", axis=0, tiled=True)
    held = lax.axis_index("replica") * requests + jnp.arange(requests, dtype=jnp.int32)
    count = all_src.shape[0]
    users = jnp.sum(
        jnp.where(all_src[None, :] == held[:, None], jnp.arange(count, dtype=jnp.int32), 0), axis=1
    )
    here = attend(pick(all_queries, users), latent_cache, cache_lengths)
    context = pick(lax.all_gather(here, "replica", axis=0, tiled=True), move_src)
    return (moe_out, context)


def solution(mesh):
    return jax.shard_map(
        local,
        mesh=mesh,
        in_specs=(
            P(("groups", "expert", "replica"), None),
            P(("groups", "expert", "replica"), None),
            P(("groups", "expert", "replica"), None),
            P("expert", None, "replica"),
            P("expert", None, "replica"),
            P("expert", "replica", None),
            P(("groups", "expert", "replica"), None, None),
            P(("groups", "expert", "replica"), None, None),
            P(("groups", "expert", "replica")),
            P(("groups", "expert", "replica")),
        ),
        out_specs=(
            P(("groups", "expert", "replica"), None),
            P(("groups", "expert", "replica"), None, None),
        ),
        check_vma=False,
    )
```

time: 271 us -> 137 us (0.51)
  waiting for transfers between devices: 121 us -> 9.29 us
  local copies, waits for them, and re-layouts: 35.2 us -> 5.81 us
  matrix products: 57.8 us -> 34.5 us
  blocking collectives: 33.3 us -> 50.4 us
  between operations: 14.5 us -> 30.3 us
    reduce_scatter x1 -> x0, waiting for transfers between devices: 58.9 us -> none  [local(): lax.psum_scatter(partials, 'replica', scatter_dimension=0, tiled=True)]
    all_gather x2, waiting for transfers between devices: 61.6 us -> 8.59 us  [the longest x1 8.59 us: local(): lax.all_gather(here, 'replica', axis=0, tiled=True)]
    all_gather x0 -> x2, blocking collectives: none -> 44.4 us  [the longest x1 26.9 us: local(): rows = lax.all_gather(moe_rows, both, axis=0, tiled=True)]
    all_to_all x1 -> x0, blocking collectives: 29 us -> none  [local(): lax.all_to_all(outgoing, 'expert', split_axis=0, concat_axis=0, tiled=True)]
    dot_general x5 -> x2, matrix products: 56 us -> 32.9 us  [the longest x1 20.9 us: local(): jnp.einsum('enf,efd->nd', hidden, w_down, preferred_element_type=jnp.floa...]
    transpose x1 -> x0, local copies, waits for them, and re-layouts: 10.3 us -> none  [expert_block(): jnp.einsum('senf,efd->send', hidden, w_down, preferred_element_type=jnp.f...]
    reshape x3 -> x1, local copies, waits for them, and re-layouts: 11.3 us -> 1.31 us  [local(): partial = partial.astype(jnp.bfloat16).reshape(n_dev, tokens, model_width)]
    all_gather x1 -> x0, local copies, waits for them, and re-layouts: 7.7 us -> none  [local(): piece_cache = lax.all_gather(latent_cache, 'replica', axis=0, tiled=True)]
  transfers between devices with their start and end apart: 4 -> 3, of which waited for: 3 -> 1; matrix products, arithmetic and copies ran while one was open for 11% -> 30% of each run, Pallas kernels for 0% -> 0%
where the time goes in v1:
time: 137 us
  blocking collectives  50.4 us (37%)
  matrix products  34.5 us (25%)
  between operations  30.3 us (22%)
  waiting for transfers between devices  9.29 us (7%)
  local copies, waits for them, and re-layouts  5.81 us (4%)
  starting transfers between devices  3.71 us (3%)
  other arithmetic  3 us (2%)
    all_gather x1, blocking collectives, local(): rows = lax.all_gather(moe_rows, both, axis=0, tiled=True)  26.9 us
    dot_general x1, matrix products, local(): jnp.einsum('enf,efd->nd', hidden, w_down, preferred_element_type=jnp.floa...  20.9 us
    all_gather x1, blocking collectives, local(): combine = lax.all_gather(combine, both, axis=0, tiled=True)  17.5 us
    dot_general x1, matrix products, local(): jnp.einsum('nd,edf->enf', rows, w_gate, preferred_element_type=jnp.float32)  12 us
    all_gather x1, waiting for transfers between devices, local(): lax.all_gather(here, 'replica', axis=0, tiled=True)  8.59 us
    unnamed x1, blocking collectives  5.95 us
    all_to_all x1, starting transfers between devices, local(): lax.all_to_all(partial, both, split_axis=0, concat_axis=0, tiled=True)  3.63 us
  transfers between devices with their start and end apart: 3, of which 1 were waited for; matrix products, arithmetic and copies ran while one was open for 30% of the time, Pallas kernels for 0%

profile of v1, /device:TPU:0, one launch (start us, length us, event | category | flops | bytes accessed | tf_op | source)
XLA Modules:
  0.0 136.9 jit_solution(10068511176047416758)
XLA Ops:
  7.2 0.7 all-gather.5.cloned.1.call-update
  7.9 26.9 %all-gather = bf16[16,4,7168]{2,1,0:T(4,128)(2,1)S(1)} all-gather(bf16[1,4,7168]{2,1,0:T(4,128)(2,1)} %bitcast.39), channel_id=1, replica_groups=mesh['groups'=2,'expert'=4,'replica'=4] {'expert','replica'}, dimensions={0}, use_global_device_ids=true | all-gather | bytes 974848 | tf_op jit(solution)/shard_map/all_gather | solution.py:56
  34.8 0.2 reshape.48
  35.0 0.8 select_reduce_fusion
  35.8 17.5 %all-gather.1 = f32[16,4,32]{2,1,0:T(4,128)S(1)} all-gather(f32[1,4,32]{2,1,0:T(4,128)S(1)} %bitcast.40), channel_id=1, replica_groups=mesh['groups'=2,'expert'=4,'replica'=4] {'expert','replica'}, dimensions={0}, use_global_device_ids=true | all-gather | bytes 8704 | tf_op jit(solution)/shard_map/all_gather | solution.py:57
  53.3 0.1 constant_dynamic-slice_fusion.8
  53.4 12.0 %convolution_bitcast_fusion.2 = f32[8,64,256]{2,1,0:T(8,128)S(1)} fusion(bf16[64,7168,1]{1,0,2:T(8,128)(2,1)S(1)} %reshape.48, bf16[8,7168,256]{2,1,0:T(8,128)(2,1)} %param.13), kind=kOutput, calls=%fused_computation.6 | convolution fusion | flops 1879048192 | bytes 30801920 | tf_op jit(solution)/shard_map/nd,edf->enf/dot_general | solution.py:61
  65.5 20.9 %fusion.1 = bf16[64,7168]{1,0:T(8,128)(2,1)S(1)} fusion(bf16[8,256,7168]{2,1,0:T(8,128)(2,1)} %param.15, bf16[64,7168,1]{1,0,2:T(8,128)(2,1)S(1)} %reshape.48, bf16[8,7168,256]{2,1,0:T(8,128)(2,1)} %param.14, f32[8,64,256]{2,1,0:T(8,128)S(1)} %convolution_bitcast_fusion.2, f32[8,64]{1,0:T(8,128)S(1)} %bitcast.37), kind=kOutput, calls=%fused_computation.2 | convolution fusion | flops 3759472640 | bytes 61081600 | tf_op jit(solution)/shard_map/enf,efd->nd/dot_general | solution.py:64
  86.4 1.3 reshape.38
  87.7 3.6 %all-to-all-start = ((bf16[16,4,7168]{2,1,0:T(4,128)(2,1)}), bf16[16,4,7168]{2,1,0:T(4,128)(2,1)S(1)}, u32[]{:S(2)}, u32[]{:S(2)}) async-start(bf16[16,4,7168]{2,1,0:T(4,128)(2,1)} %reshape.38), calls=%async_computation | async-start | bytes 1835008 | tf_op jit(solution)/shard_map/all_to_all | solution.py:66
  91.4 0.6 dynamic-slice
  92.7 0.2 dynamic-update-slice
  92.9 6.0 %all-reduce = s32[16]{0:T(128)S(1)} all-reduce(s32[16]{0:T(128)S(1)} %dynamic-update-slice), channel_id=1, replica_groups=mesh['groups'=2,'expert'=4,'replica'=4] {'replica'}, use_global_device_ids=true, to_apply=%add | all-reduce | flops 16 | bytes 128
  98.9 0.2 select_reduce_fusion.1
  99.1 0.7 fusion.28
  107.6 1.0 constant_dynamic-slice_fusion.7
  108.7 0.3 fusion.6
  109.0 0.2 fusion.29
  109.2 1.3 convolution_convert_fusion
  110.5 0.7 fusion.27
  118.8 1.0 reduce_sum.40
  119.8 8.6 %all-gather.7.cloned.1.call-done = bf16[16,64,512]{2,1,0:T(8,128)(2,1)} async-done(((bf16[4,64,512]{2,1,0:T(8,128)(2,1)}), bf16[16,64,512]{2,1,0:T(8,128)(2,1)}) %all-gather.7.cloned.1.call-update) | async-done | bytes 1048592 | tf_op jit(solution)/shard_map/all_gather | solution.py:78
  128.4 1.0 constant_dynamic-slice_fusion.3
  129.3 0.7 pad_maximum_fusion
  (17 shorter events, 0.3 us)
Async XLA Ops:
  7.2 100.5 %all-gather.5.cloned.1.call-start = ((), (), s32[]{:S(2)}) async-start(), calls=%async_computation.1 | async-start | bytes 1638400 | tf_op jit(solution)/shard_map/all_gather | solution.py:70
  65.4 26.0 %copy-start.3 = (u32[32]{0:T(128)S(1)}, u32[32]{0:T(128)}, u32[]{:S(2)}) copy-start(u32[32]{0:T(128)} %constant.37) | copy-start | bytes 388
  65.5 27.2 %copy-start = (s32[4]{0:T(128)S(1)}, s32[4]{0:T(128)}, u32[]{:S(2)}) copy-start(s32[4]{0:T(128)} %param.19) | copy-start | bytes 52
  65.5 42.1 %copy-start.2 = (s32[4]{0:T(128)S(1)}, s32[4]{0:T(128)}, u32[]{:S(2)}) copy-start(s32[4]{0:T(128)} %param.18) | copy-start | bytes 52
  65.5 43.2 %copy-start.1 = (bf16[4,256,576]{1,2,0:T(8,128)(2,1)S(1)}, bf16[4,256,576]{1,2,0:T(8,128)(2,1)}, u32[]{:S(2)}) copy-start(bf16[4,256,576]{1,2,0:T(8,128)(2,1)} %param.17) | copy-start | bytes 3538948
  87.7 31.1 %all-to-all-start = ((bf16[16,4,7168]{2,1,0:T(4,128)(2,1)}), bf16[16,4,7168]{2,1,0:T(4,128)(2,1)S(1)}, u32[]{:S(2)}, u32[]{:S(2)}) async-start(bf16[16,4,7168]{2,1,0:T(4,128)(2,1)} %reshape.38), calls=%async_computation | async-start | bytes 1835008 | tf_op jit(solution)/shard_map/all_to_all | solution.py:66
  91.3 37.0 %all-gather.7.cloned.1.call-start = ((), (), s32[]{:S(2)}) async-start(), calls=%async_computation.2 | async-start | bytes 1310720 | tf_op jit(solution)/shard_map/all_gather | solution.py:78
Sparse Core Ops, SparseCore 0:
  9.6 24.9 all-gather.4
  110.6 17.7 all-gather.6

commit v2 on v1

--- a/solution.py
+++ b/solution.py
@@ -1,6 +1,10 @@
+import functools
+
 import jax
 import jax.numpy as jnp
 from jax import lax
+from jax.experimental import pallas as pl
+from jax.experimental.pallas import tpu as pltpu
 from jax.sharding import PartitionSpec as P
 
 LAT = 512
@@ -32,7 +36,7 @@
     )
 
 
-def local(
+def by_collectives(
     moe_rows,
     expert_ids,
     expert_weights,
@@ -79,6 +83,472 @@
     return (moe_out, context)
 
 
+MESH = pl.DeviceIdType.MESH
+CHUNKS = 8
+DEPTH = 4
+DOWN_DEPTH = 3
+
+
+def fused_kernel(
+    n_expert,
+    lengths_ref,
+    own_src_ref,
+    src_ref,
+    rows_ref,
+    queries_ref,
+    cache_ref,
+    wg_ref,
+    wu_ref,
+    wd_ref,
+    out_ref,
+    context_ref,
+    rows_all,
+    x32,
+    xb,
+    gate_buf,
+    up_buf,
+    down_buf,
+    hid,
+    y,
+    sum_a,
+    send_b,
+    sum_b,
+    y16,
+    send_c,
+    sum_c,
+    q_all,
+    src_all,
+    src_smem,
+    ctx_all,
+    gate_sem,
+    up_sem,
+    down_sem,
+    row_send_z,
+    row_send_2,
+    row_send_1,
+    row_recv,
+    q_send,
+    q_recv,
+    src_send,
+    src_recv,
+    src_local,
+    ctx_send,
+    ctx_recv,
+    a_send,
+    a_recv,
+    b_send,
+    b_recv,
+    c_send,
+    c_recv,
+):
+    me_e = lax.axis_index("expert")
+    me_r = lax.axis_index("replica")
+    r2 = (me_r + 2) % 4
+    r1 = me_r + 1 - 2 * (me_r % 2)
+    r3 = (r1 + 2) % 4
+    tokens = rows_ref.shape[0]
+    local_experts, width, ff = wg_ref.shape
+    experts = local_experts * n_expert
+    chunk = width // CHUNKS
+    band = n_expert * tokens
+    requests = queries_ref.shape[0]
+
+    def gate_copy(e):
+        return pltpu.make_async_copy(
+            wg_ref.at[e], gate_buf.at[e % DEPTH], gate_sem.at[e % DEPTH]
+        )
+
+    def up_copy(e):
+        return pltpu.make_async_copy(wu_ref.at[e], up_buf.at[e % DEPTH], up_sem.at[e % DEPTH])
+
+    def down_copy(c):
+        return pltpu.make_async_copy(
+            wd_ref.at[:, :, pl.ds(pl.multiple_of(c * chunk, 128), chunk)],
+            down_buf.at[c % DOWN_DEPTH],
+            down_sem.at[c % DOWN_DEPTH],
+        )
+
+    for e in range(DEPTH):
+        gate_copy(e).start()
+        up_copy(e).start()
+    for c in range(DOWN_DEPTH):
+        down_copy(c).start()
+
+    barrier = pltpu.get_barrier_semaphore()
+    for d in range(1, n_expert):
+        pl.semaphore_signal(
+            barrier, inc=1, device_id={"expert": (me_e + d) % n_expert}, device_id_type=MESH
+        )
+    for r in (r2, r1):
+        pl.semaphore_signal(barrier, inc=1, device_id={"replica": r}, device_id_type=MESH)
+    pl.semaphore_wait(barrier, n_expert + 1)
+
+    def remote(src, dst, send, recv, **where):
+        return pltpu.make_async_remote_copy(
+            src_ref=src,
+            dst_ref=dst,
+            send_sem=send,
+            recv_sem=recv,
+            device_id=where,
+            device_id_type=MESH,
+        )
+
+    def slot(e, r):
+        return rows_all.at[e * 4 + r]
+
+    def row_z(d):
+        mine = me_e * 4 + me_r
+        return remote(
+            rows_ref,
+            rows_all.at[mine],
+            row_send_z.at[d - 1],
+            row_recv.at[mine],
+            expert=(me_e + d) % n_expert,
+        )
+
+    def row_to(d, r, source, sems, src=None):
+        at = ((me_e + d) % n_expert) * 4 + source
+        return remote(
+            rows_all.at[at] if src is None else src,
+            rows_all.at[at],
+            sems,
+            row_recv.at[at],
+            replica=r,
+        )
+
+    def arrived(at):
+        return remote(
+            rows_all.at[at], rows_all.at[at], row_send_z.at[0], row_recv.at[at], replica=r1
+        )
+
+    def block(ref, r):
+        return ref.at[pl.ds(pl.multiple_of(r * requests, requests), requests)]
+
+    sends = []
+
+    def go(copy):
+        copy.start()
+        sends.append(copy)
+
+    for d in range(1, n_expert):
+        go(row_z(d))
+    go(row_to(0, r2, me_r, row_send_2.at[0], rows_ref))
+    go(row_to(0, r1, me_r, row_send_1.at[0], rows_ref))
+    for i, r in enumerate((r2, r1)):
+        go(remote(src_ref, src_all.at[me_r], src_send.at[i], src_recv.at[me_r], replica=r))
+    rows_all[me_e * 4 + me_r] = rows_ref[...]
+    src_all[me_r] = src_ref[...]
+    q_all[pl.ds(me_r * requests, requests)] = queries_ref[...]
+    for d in range(1, n_expert):
+        arrived(((me_e + d) % n_expert) * 4 + me_r).wait_recv()
+        go(row_to(d, r2, me_r, row_send_2.at[d]))
+        go(row_to(d, r1, me_r, row_send_1.at[d]))
+    for i, r in enumerate((r2, r1)):
+        go(remote(queries_ref, block(q_all, me_r), q_send.at[i], q_recv.at[me_r], replica=r))
+    for d in range(n_expert):
+        arrived(((me_e + d) % n_expert) * 4 + r2).wait_recv()
+        go(row_to(d, r1, r2, row_send_1.at[n_expert + d]))
+    pltpu.make_async_copy(src_all.at[r2], src_all.at[r2], src_recv.at[r2]).wait()
+    go(remote(src_all.at[r2], src_all.at[r2], src_send.at[2], src_recv.at[r2], replica=r1))
+    for r in (r1, r3):
+        for d in range(n_expert):
+            arrived(((me_e + d) % n_expert) * 4 + r).wait_recv()
+
+    for k, r in enumerate((me_r, r2, r1, r3)):
+        for e in range(n_expert):
+            x32[e * tokens : (e + 1) * tokens, :] = rows_all[e * 4 + r].astype(jnp.float32)
+        xb[k * band : (k + 1) * band, :] = x32[...].astype(jnp.bfloat16)
+
+    places = lax.broadcasted_iota(jnp.int32, (128, ff), 0)
+
+    def first(e, carry):
+        gate_copy(e).wait()
+        up_copy(e).wait()
+        x = xb[:, :width]
+        gate = jnp.dot(x, gate_buf[e % DEPTH], preferred_element_type=jnp.float32)
+        up = jnp.dot(x, up_buf[e % DEPTH], preferred_element_type=jnp.float32)
+        mine = me_e * local_experts + e
+        hit = (places == mine) | (places == mine + experts) | (places == mine + 2 * experts)
+        weight = jnp.dot(
+            xb[:, width:],
+            jnp.where(hit, 1.0, 0.0).astype(jnp.bfloat16),
+            preferred_element_type=jnp.float32,
+        )
+        hidden = (gate / (1.0 + jnp.exp(-gate)) * up).astype(jnp.bfloat16)
+        hid[e] = (hidden.astype(jnp.float32) * weight).astype(jnp.bfloat16)
+
+        @pl.when(e + DEPTH < local_experts)
+        def _():
+            gate_copy(e + DEPTH).start()
+            up_copy(e + DEPTH).start()
+
+        return carry
+
+    def q_forward():
+        return remote(
+            block(q_all, r2), block(q_all, r2), q_send.at[2], q_recv.at[r2], replica=r1
+        )
+
+    half = local_experts // 2
+    lax.fori_loop(0, half, first, 0)
+    q_forward().wait_recv()
+    go(q_forward())
+    for r in (r1, r3):
+        pltpu.make_async_copy(src_all.at[r], src_all.at[r], src_recv.at[r]).wait()
+    local_src = pltpu.make_async_copy(src_all, src_smem, src_local)
+    local_src.start()
+    lax.fori_loop(half, local_experts, first, 0)
+    local_src.wait()
+    for r in (r1, r3):
+        remote(block(q_all, r), block(q_all, r), q_send.at[0], q_recv.at[r], replica=r1).wait_recv()
+
+    positions = cache_ref.shape[1]
+    seen = lax.broadcasted_iota(jnp.int32, (queries_ref.shape[1], positions), 1)
+    for j in range(requests):
+        held = me_r * requests + j
+        user = jnp.int32(0)
+        for r in range(4):
+            for i in range(requests):
+                user = jnp.where(src_smem[r, 0, i] == held, r * requests + i, user)
+        scores = (
+            lax.dot_general(
+                q_all[user],
+                cache_ref[j],
+                (((1,), (1,)), ((), ())),
+                preferred_element_type=jnp.float32,
+            )
+            * score_scale
+        )
+        scores = jnp.where(seen < lengths_ref[j], scores, -jnp.inf)
+        powers = jnp.exp(scores - jnp.max(scores, axis=1, keepdims=True))
+        probs = (powers / jnp.sum(powers, axis=1, keepdims=True)).astype(jnp.bfloat16)
+        ctx_all[me_r * requests + j] = jnp.dot(
+            probs, cache_ref[j, :, :LAT], preferred_element_type=jnp.float32
+        ).astype(jnp.bfloat16)
+    for i, r in enumerate((r2, r1)):
+        go(
+            remote(
+                block(ctx_all, me_r),
+                block(ctx_all, me_r),
+                ctx_send.at[i],
+                ctx_recv.at[me_r],
+                replica=r,
+            )
+        )
+
+    def a_copy(c):
+        return remote(
+            y.at[c, pl.ds(2 * band, 2 * band)], sum_a.at[c], a_send.at[c], a_recv.at[c], replica=r1
+        )
+
+    def b_copy(c):
+        return remote(send_b.at[c], sum_b.at[c], b_send.at[c], b_recv.at[c], replica=r2)
+
+    def c_copy(c, d):
+        to = (me_e + d) % n_expert
+        return remote(
+            send_c.at[c, to],
+            sum_c.at[c, me_e],
+            c_send.at[c, d - 1],
+            c_recv.at[c, me_e],
+            expert=to,
+        )
+
+    def c_arrived(c, d):
+        at = (me_e + d) % n_expert
+        return remote(
+            send_c.at[c, at], sum_c.at[c, at], c_send.at[c, d - 1], c_recv.at[c, at], expert=at
+        )
+
+    def second(step, carry):
+        @pl.when(step < CHUNKS)
+        def _():
+            down_copy(step).wait()
+            total = jnp.dot(
+                hid[0], down_buf[step % DOWN_DEPTH, 0], preferred_element_type=jnp.float32
+            )
+            for e in range(1, local_experts):
+                total += jnp.dot(
+                    hid[e], down_buf[step % DOWN_DEPTH, e], preferred_element_type=jnp.float32
+                )
+            y[step] = total
+            a_copy(step).start()
+
+            @pl.when(step + DOWN_DEPTH < CHUNKS)
+            def _():
+                down_copy(step + DOWN_DEPTH).start()
+
+        @pl.when((step >= 1) & (step <= CHUNKS))
+        def _():
+            c = step - 1
+            a_copy(c).wait_recv()
+            send_b[c] = (y[c, band : 2 * band] + sum_a[c, band:]).astype(jnp.bfloat16)
+            b_copy(c).start()
+
+        @pl.when(step >= 2)
+        def _():
+            c = step - 2
+            b_copy(c).wait_recv()
+            y16[...] = y[c, :band] + sum_a[c, :band] + sum_b[c].astype(jnp.float32)
+            for e in range(n_expert):
+                send_c[c, e] = y16[e * tokens : (e + 1) * tokens].astype(jnp.bfloat16)
+            for d in range(1, n_expert):
+                c_copy(c, d).start()
+
+        return carry
+
+    def ctx_forward():
+        return remote(
+            block(ctx_all, r2), block(ctx_all, r2), ctx_send.at[2], ctx_recv.at[r2], replica=r1
+        )
+
+    lax.fori_loop(0, CHUNKS - 1, second, 0)
+    ctx_forward().wait_recv()
+    go(ctx_forward())
+    lax.fori_loop(CHUNKS - 1, CHUNKS + 2, second, 0)
+
+    for r in (r1, r3):
+        remote(
+            block(ctx_all, r), block(ctx_all, r), ctx_send.at[0], ctx_recv.at[r], replica=r1
+        ).wait_recv()
+    for j in range(requests):
+        context_ref[j] = ctx_all[own_src_ref[j]]
+    for c in range(CHUNKS):
+        total = send_c[c, me_e].astype(jnp.float32)
+        for d in range(1, n_expert):
+            c_arrived(c, d).wait_recv()
+            total += sum_c[c, (me_e + d) % n_expert].astype(jnp.float32)
+        out_ref[:, c * chunk : (c + 1) * chunk] = total.astype(jnp.bfloat16)
+
+    for copy in sends:
+        copy.wait_send()
+
+    def drain(c, carry):
+        a_copy(c).wait_send()
+        b_copy(c).wait_send()
+        for d in range(1, n_expert):
+            c_copy(c, d).wait_send()
+        return carry
+
+    lax.fori_loop(0, CHUNKS, drain, 0)
+
+
+def fused(
+    moe_rows,
+    expert_ids,
+    expert_weights,
+    w_gate,
+    w_up,
+    w_down,
+    queries,
+    latent_cache,
+    cache_lengths,
+    move_src,
+):
+    n_expert = lax.axis_size("expert")
+    tokens = expert_ids.shape[0]
+    local_experts, width, ff = w_gate.shape
+    experts = local_experts * n_expert
+    requests, heads, channels = queries.shape
+    onehot = expert_ids[:, :, None] == jnp.arange(experts, dtype=jnp.int32)
+    combine = jnp.sum(jnp.where(onehot, expert_weights[:, :, None], 0.0), axis=1)
+    pieces = []
+    rest = combine
+    for _ in range(3):
+        piece = lax.reduce_precision(rest, 8, 7)
+        pieces.append(piece.astype(jnp.bfloat16))
+        rest = rest - piece
+    spare = 128 - 3 * experts
+    rows = jnp.concatenate(
+        [moe_rows] + pieces + [jnp.zeros((tokens, spare), jnp.bfloat16)], axis=1
+    )
+    src_block = jnp.zeros((8, 128), jnp.int32).at[0, :requests].set(move_src)
+    chunk = width // CHUNKS
+    band = n_expert * tokens
+    n = 4 * band
+    bf16, f32 = jnp.bfloat16, jnp.float32
+    vmem = pl.BlockSpec(memory_space=pltpu.VMEM)
+    smem = pl.BlockSpec(memory_space=pltpu.SMEM)
+    hbm = pl.BlockSpec(memory_space=pl.ANY)
+    dma = pltpu.SemaphoreType.DMA
+    return pl.pallas_call(
+        functools.partial(fused_kernel, n_expert),
+        out_shape=(
+            jax.ShapeDtypeStruct((tokens, width), bf16),
+            jax.ShapeDtypeStruct((requests, heads, LAT), bf16),
+        ),
+        in_specs=[smem, smem, vmem, vmem, vmem, vmem, hbm, hbm, hbm],
+        out_specs=(vmem, vmem),
+        scratch_shapes=[
+            pltpu.VMEM((4 * n_expert, tokens, width + 128), bf16),
+            pltpu.VMEM((band, width + 128), f32),
+            pltpu.VMEM((n, width + 128), bf16),
+            pltpu.VMEM((DEPTH, width, ff), bf16),
+            pltpu.VMEM((DEPTH, width, ff), bf16),
+            pltpu.VMEM((DOWN_DEPTH, local_experts, ff, chunk), bf16),
+            pltpu.VMEM((local_experts, n, ff), bf16),
+            pltpu.VMEM((CHUNKS, n, chunk), f32),
+            pltpu.VMEM((CHUNKS, 2 * band, chunk), f32),
+            pltpu.VMEM((CHUNKS, band, chunk), bf16),
+            pltpu.VMEM((CHUNKS, band, chunk), bf16),
+            pltpu.VMEM((band, chunk), f32),
+            pltpu.VMEM((CHUNKS, n_expert, tokens, chunk), bf16),
+            pltpu.VMEM((CHUNKS, n_expert, tokens, chunk), bf16),
+            pltpu.VMEM((4 * requests, heads, channels), bf16),
+            pltpu.VMEM((4, 8, 128), jnp.int32),
+            pltpu.SMEM((4, 8, 128), jnp.int32),
+            pltpu.VMEM((4 * requests, heads, LAT), bf16),
+            dma((DEPTH,)),
+            dma((DEPTH,)),
+            dma((DOWN_DEPTH,)),
+            dma((n_expert,)),
+            dma((n_expert,)),
+            dma((2 * n_expert,)),
+            dma((4 * n_expert,)),
+            dma((3,)),
+            dma((4,)),
+            dma((3,)),
+            dma((4,)),
+            dma,
+            dma((3,)),
+            dma((4,)),
+            dma((CHUNKS,)),
+            dma((CHUNKS,)),
+            dma((CHUNKS,)),
+            dma((CHUNKS,)),
+            dma((CHUNKS, n_expert)),
+            dma((CHUNKS, n_expert)),
+        ],
+        compiler_params=pltpu.CompilerParams(
+            collective_id=0, has_side_effects=True, vmem_limit_bytes=62 * 1024 * 1024
+        ),
+    )(
+        cache_lengths,
+        move_src,
+        src_block,
+        rows,
+        queries,
+        latent_cache,
+        w_gate,
+        w_up,
+        w_down,
+    )
+
+
+def local(*arrays):
+    n_expert, n_replica = lax.axis_size("expert"), lax.axis_size("replica")
+    tokens = arrays[0].shape[0]
+    local_experts = arrays[3].shape[0]
+    small = (
+        n_replica == 4
+        and n_expert * tokens == 16
+        and local_experts >= DEPTH
+        and local_experts % 2 == 0
+        and 3 * local_experts * n_expert <= 128
+    )
+    return fused(*arrays) if small else by_collectives(*arrays)
+
+
 def solution(mesh):
     return jax.shard_map(
         local,

time: 137 us -> 70.5 us (0.51)
  Pallas kernels: 0 us -> 60.4 us
  blocking collectives: 50.4 us -> 0 us
  matrix products: 34.5 us -> 0 us
  between operations: 30.3 us -> 0.64 us
  waiting for transfers between devices: 9.29 us -> 0 us
  starting transfers between devices: 3.71 us -> 0 us
  local copies, waits for them, and re-layouts: 5.81 us -> 8.33 us
  other arithmetic: 3 us -> 0.8 us
    pallas_call x0 -> x1, Pallas kernels: none -> 60.4 us  [fused(): pl.pallas_call(functools.partial(fused_kernel, n_expert), out_shape=(jax....]
    all_gather x2 -> x0, blocking collectives: 44.4 us -> none  [the longest x1 26.9 us: local(): rows = lax.all_gather(moe_rows, both, axis=0, tiled=True)]
    dot_general x4 -> x0, matrix products: 34.5 us -> none  [the longest x1 20.9 us: local(): jnp.einsum('enf,efd->nd', hidden, w_down, preferred_element_type=jnp.floa...]
    all_gather x2 -> x0, waiting for transfers between devices: 8.59 us -> none  [the longest x1 8.59 us: local(): lax.all_gather(here, 'replica', axis=0, tiled=True)]
    unnamed x1 -> x0, blocking collectives: 5.95 us -> none
    unnamed x13 -> x3, local copies, waits for them, and re-layouts: 1.12 us -> 5.55 us
    all_to_all x1 -> x0, starting transfers between devices: 3.63 us -> none  [local(): lax.all_to_all(partial, both, split_axis=0, concat_axis=0, tiled=True)]
    dynamic_slice x3 -> x0, local copies, waits for them, and re-layouts: 2.06 us -> none  [the longest x2 1.99 us: pick(): lax.dynamic_slice_in_dim(stack, places[i], 1, axis=0)]
  transfers between devices with their start and end apart: 3 -> 0, of which waited for: 1 -> 0; matrix products, arithmetic and copies ran while one was open for 30% -> 0% of each run, Pallas kernels for 0% -> 0%
where the time goes in v2:
time: 70.5 us; the launch traced here: 70.2 us
  Pallas kernels  60.4 us (86%)
  local copies, waits for them, and re-layouts  8.33 us (12%)
  other arithmetic  0.8 us (1%)
    pallas_call x1, Pallas kernels, fused(): pl.pallas_call(functools.partial(fused_kernel, n_expert), out_shape=(jax....  60.4 us
    unnamed x3, local copies, waits for them, and re-layouts  5.55 us
    concatenate x1, local copies, waits for them, and re-layouts, fused(): jnp.concatenate([moe_rows] + pieces + [jnp.zeros((tokens, spare), jnp.bfl...  1.53 us

profile of v2, /device:TPU:0, one launch (start us, length us, event | category | flops | bytes accessed | tf_op | source)
XLA Modules:
  0.0 70.2 jit_solution(5878508945685771423)
XLA Ops:
  0.6 0.8 %select_reduce_fusion = f32[4,32]{1,0:T(4,128)S(1)} fusion(f32[4,8]{1,0:T(4,128)} %param.14, s32[4,8]{1,0:T(4,128)} %param.13), kind=kLoop, calls=%fused_computation | loop fusion | flops 2944 | bytes 768 | tf_op jit(solution)/shard_map/reduce_sum | solution.py:454
  1.4 1.3 %scatter.4.src_ref = s32[8,128]{1,0:T(8,128)} pad(s32[1,4]{1,0:T(1,128)} %bitcast.1, s32[]{:T(128)} %constant.28.clone.1), padding=0_7x0_124 | pad | bytes 4116 | tf_op jit(solution)/shard_map/scatter | solution.py:465
  2.7 1.5 %concatenate.5.rows_ref = bf16[4,7296]{1,0:T(4,128)(2,1)} concatenate(bf16[4,7168]{1,0:T(4,128)(2,1)} %param.12, bf16[4,32]{1,0:T(4,128)(2,1)S(1)} %get-tuple-element.16, bf16[4,32]{1,0:T(4,128)(2,1)S(1)} %get-tuple-element.15, bf16[4,32]{1,0:T(4,128)(2,1)S(1)} %get-tuple-element.14, bf16[4,32]{1,0:T(4,128)(2,1)S(1)} %broadcast_in_dim.21), dimensions={1} | concatenate | bytes 116736 | tf_op jit(solution)/shard_map/concatenate | solution.py:462
  4.2 2.4 %copy.13.cache_ref = bf16[4,256,576]{2,1,0:T(8,128)(2,1)} copy(bf16[4,256,576]{1,2,0:T(8,128)(2,1)} %param.19) | data formatting | bytes 2359296 | tf_op args[7]
  6.6 60.4 %shard_map.113 = (bf16[4,7168]{1,0:T(4,128)(2,1)}, bf16[4,64,512]{2,1,0:T(8,128)(2,1)}) custom-call(s32[4]{0:T(128)} %lengths_ref.1, s32[4]{0:T(128)} %own_src_ref.1, s32[8,128]{1,0:T(8,128)} %scatter.4.src_ref, bf16[4,7296]{1,0:T(4,128)(2,1)} %concatenate.5.rows_ref, bf16[4,64,576]{2,1,0:T(8,128)(2,1)} %queries_ref.1, bf16[4,256,576]{2,1,0:T(8,128)(2,1)} %copy.13.cache_ref, ...), custom_call_target="tpu_custom_call" | custom-call | tf_op jit(solution)/shard_map/pallas_call | solution.py:474
  67.0 1.5 %copy.16 = bf16[4,7168]{1,0:T(4,128)(2,1)} copy(bf16[4,7168]{1,0:T(4,128)(2,1)} %get-tuple-element.19) | data formatting | bytes 114688
  68.5 1.7 %copy.17 = bf16[4,64,512]{2,1,0:T(8,128)(2,1)} copy(bf16[4,64,512]{2,1,0:T(8,128)(2,1)} %get-tuple-element.20) | data formatting | bytes 524288
  (2 shorter events, 0.0 us)

commit v3 on v2

--- a/solution.py
+++ b/solution.py
@@ -87,16 +87,18 @@
 CHUNKS = 8
 DEPTH = 4
 DOWN_DEPTH = 3
+LAG = 2
 
 
 def fused_kernel(
     n_expert,
     lengths_ref,
     own_src_ref,
-    src_ref,
+    ids_ref,
+    weights_ref,
     rows_ref,
     queries_ref,
-    cache_ref,
+    cache_hbm,
     wg_ref,
     wu_ref,
     wd_ref,
@@ -120,6 +122,9 @@
     src_all,
     src_smem,
     ctx_all,
+    cache_ref,
+    q_local,
+    cache_local,
     gate_sem,
     up_sem,
     down_sem,
@@ -168,11 +173,41 @@
             down_sem.at[c % DOWN_DEPTH],
         )
 
+    own_q = pltpu.make_async_copy(
+        queries_ref,
+        q_all.at[pl.ds(pl.multiple_of(me_r * requests, requests), requests)],
+        q_local,
+    )
+    own_cache = pltpu.make_async_copy(cache_hbm, cache_ref, cache_local)
+    own_q.start()
+    own_cache.start()
     for e in range(DEPTH):
         gate_copy(e).start()
         up_copy(e).start()
     for c in range(DOWN_DEPTH):
         down_copy(c).start()
+
+    mine = me_e * 4 + me_r
+    lane = lax.broadcasted_iota(jnp.int32, (tokens, 128), 1)
+    expert = lane % experts
+    combine = jnp.zeros((tokens, 128), jnp.float32)
+    for k in range(ids_ref.shape[1]):
+        combine += jnp.where(ids_ref[:, k : k + 1] == expert, weights_ref[:, k : k + 1], 0.0)
+    high = combine.astype(jnp.bfloat16).astype(jnp.float32)
+    middle = (combine - high).astype(jnp.bfloat16).astype(jnp.float32)
+    low = combine - high - middle
+    pieces = jnp.where(
+        lane < experts,
+        high,
+        jnp.where(lane < 2 * experts, middle, jnp.where(lane < 3 * experts, low, 0.0)),
+    )
+    rows_all[mine, :, :width] = rows_ref[...]
+    rows_all[mine, :, width:] = pieces.astype(jnp.bfloat16)
+    place = lax.broadcasted_iota(jnp.int32, (8, 128), 1)
+    sources = jnp.zeros((8, 128), jnp.int32)
+    for i in range(requests):
+        sources = jnp.where(place == i, own_src_ref[i], sources)
+    src_all[me_r] = sources
 
     barrier = pltpu.get_barrier_semaphore()
     for d in range(1, n_expert):
@@ -197,19 +232,18 @@
         return rows_all.at[e * 4 + r]
 
     def row_z(d):
-        mine = me_e * 4 + me_r
-        return remote(
-            rows_ref,
+        return remote(
+            rows_all.at[mine],
             rows_all.at[mine],
             row_send_z.at[d - 1],
             row_recv.at[mine],
             expert=(me_e + d) % n_expert,
         )
 
-    def row_to(d, r, source, sems, src=None):
+    def row_to(d, r, source, sems):
         at = ((me_e + d) % n_expert) * 4 + source
         return remote(
-            rows_all.at[at] if src is None else src,
+            rows_all.at[at],
             rows_all.at[at],
             sems,
             row_recv.at[at],
@@ -232,19 +266,17 @@
 
     for d in range(1, n_expert):
         go(row_z(d))
-    go(row_to(0, r2, me_r, row_send_2.at[0], rows_ref))
-    go(row_to(0, r1, me_r, row_send_1.at[0], rows_ref))
+    go(row_to(0, r2, me_r, row_send_2.at[0]))
+    go(row_to(0, r1, me_r, row_send_1.at[0]))
     for i, r in enumerate((r2, r1)):
-        go(remote(src_ref, src_all.at[me_r], src_send.at[i], src_recv.at[me_r], replica=r))
-    rows_all[me_e * 4 + me_r] = rows_ref[...]
-    src_all[me_r] = src_ref[...]
-    q_all[pl.ds(me_r * requests, requests)] = queries_ref[...]
+        go(remote(src_all.at[me_r], src_all.at[me_r], src_send.at[i], src_recv.at[me_r], replica=r))
     for d in range(1, n_expert):
         arrived(((me_e + d) % n_expert) * 4 + me_r).wait_recv()
         go(row_to(d, r2, me_r, row_send_2.at[d]))
         go(row_to(d, r1, me_r, row_send_1.at[d]))
+    own_q.wait()
     for i, r in enumerate((r2, r1)):
-        go(remote(queries_ref, block(q_all, me_r), q_send.at[i], q_recv.at[me_r], replica=r))
+        go(remote(block(q_all, me_r), block(q_all, me_r), q_send.at[i], q_recv.at[me_r], replica=r))
     for d in range(n_expert):
         arrived(((me_e + d) % n_expert) * 4 + r2).wait_recv()
         go(row_to(d, r1, r2, row_send_1.at[n_expert + d]))
@@ -267,8 +299,8 @@
         x = xb[:, :width]
         gate = jnp.dot(x, gate_buf[e % DEPTH], preferred_element_type=jnp.float32)
         up = jnp.dot(x, up_buf[e % DEPTH], preferred_element_type=jnp.float32)
-        mine = me_e * local_experts + e
-        hit = (places == mine) | (places == mine + experts) | (places == mine + 2 * experts)
+        at = me_e * local_experts + e
+        hit = (places == at) | (places == at + experts) | (places == at + 2 * experts)
         weight = jnp.dot(
             xb[:, width:],
             jnp.where(hit, 1.0, 0.0).astype(jnp.bfloat16),
@@ -302,7 +334,8 @@
     for r in (r1, r3):
         remote(block(q_all, r), block(q_all, r), q_send.at[0], q_recv.at[r], replica=r1).wait_recv()
 
-    positions = cache_ref.shape[1]
+    own_cache.wait()
+    positions = cache_ref.shape[2]
     seen = lax.broadcasted_iota(jnp.int32, (queries_ref.shape[1], positions), 1)
     for j in range(requests):
         held = me_r * requests + j
@@ -314,7 +347,7 @@
             lax.dot_general(
                 q_all[user],
                 cache_ref[j],
-                (((1,), (1,)), ((), ())),
+                (((1,), (0,)), ((), ())),
                 preferred_element_type=jnp.float32,
             )
             * score_scale
@@ -322,8 +355,11 @@
         scores = jnp.where(seen < lengths_ref[j], scores, -jnp.inf)
         powers = jnp.exp(scores - jnp.max(scores, axis=1, keepdims=True))
         probs = (powers / jnp.sum(powers, axis=1, keepdims=True)).astype(jnp.bfloat16)
-        ctx_all[me_r * requests + j] = jnp.dot(
-            probs, cache_ref[j, :, :LAT], preferred_element_type=jnp.float32
+        ctx_all[me_r * requests + j] = lax.dot_general(
+            probs,
+            cache_ref[j, :LAT, :],
+            (((1,), (1,)), ((), ())),
+            preferred_element_type=jnp.float32,
         ).astype(jnp.bfloat16)
     for i, r in enumerate((r2, r1)):
         go(
@@ -378,16 +414,16 @@
             def _():
                 down_copy(step + DOWN_DEPTH).start()
 
-        @pl.when((step >= 1) & (step <= CHUNKS))
+        @pl.when((step >= LAG) & (step < CHUNKS + LAG))
         def _():
-            c = step - 1
+            c = step - LAG
             a_copy(c).wait_recv()
             send_b[c] = (y[c, band : 2 * band] + sum_a[c, band:]).astype(jnp.bfloat16)
             b_copy(c).start()
 
-        @pl.when(step >= 2)
+        @pl.when(step >= 2 * LAG)
         def _():
-            c = step - 2
+            c = step - 2 * LAG
             b_copy(c).wait_recv()
             y16[...] = y[c, :band] + sum_a[c, :band] + sum_b[c].astype(jnp.float32)
             for e in range(n_expert):
@@ -405,7 +441,7 @@
     lax.fori_loop(0, CHUNKS - 1, second, 0)
     ctx_forward().wait_recv()
     go(ctx_forward())
-    lax.fori_loop(CHUNKS - 1, CHUNKS + 2, second, 0)
+    lax.fori_loop(CHUNKS - 1, CHUNKS + 2 * LAG, second, 0)
 
     for r in (r1, r3):
         remote(
@@ -448,21 +484,7 @@
     n_expert = lax.axis_size("expert")
     tokens = expert_ids.shape[0]
     local_experts, width, ff = w_gate.shape
-    experts = local_experts * n_expert
     requests, heads, channels = queries.shape
-    onehot = expert_ids[:, :, None] == jnp.arange(experts, dtype=jnp.int32)
-    combine = jnp.sum(jnp.where(onehot, expert_weights[:, :, None], 0.0), axis=1)
-    pieces = []
-    rest = combine
-    for _ in range(3):
-        piece = lax.reduce_precision(rest, 8, 7)
-        pieces.append(piece.astype(jnp.bfloat16))
-        rest = rest - piece
-    spare = 128 - 3 * experts
-    rows = jnp.concatenate(
-        [moe_rows] + pieces + [jnp.zeros((tokens, spare), jnp.bfloat16)], axis=1
-    )
-    src_block = jnp.zeros((8, 128), jnp.int32).at[0, :requests].set(move_src)
     chunk = width // CHUNKS
     band = n_expert * tokens
     n = 4 * band
@@ -477,7 +499,7 @@
             jax.ShapeDtypeStruct((tokens, width), bf16),
             jax.ShapeDtypeStruct((requests, heads, LAT), bf16),
         ),
-        in_specs=[smem, smem, vmem, vmem, vmem, vmem, hbm, hbm, hbm],
+        in_specs=[smem, smem, vmem, vmem, vmem, hbm, hbm, hbm, hbm, hbm],
         out_specs=(vmem, vmem),
         scratch_shapes=[
             pltpu.VMEM((4 * n_expert, tokens, width + 128), bf16),
@@ -498,6 +520,9 @@
             pltpu.VMEM((4, 8, 128), jnp.int32),
             pltpu.SMEM((4, 8, 128), jnp.int32),
             pltpu.VMEM((4 * requests, heads, LAT), bf16),
+            pltpu.VMEM((requests, channels, latent_cache.shape[1]), bf16),
+            dma,
+            dma,
             dma((DEPTH,)),
             dma((DEPTH,)),
             dma((DOWN_DEPTH,)),
@@ -525,10 +550,11 @@
     )(
         cache_lengths,
         move_src,
-        src_block,
-        rows,
+        expert_ids,
+        expert_weights,
+        moe_rows,
         queries,
-        latent_cache,
+        jnp.swapaxes(latent_cache, 1, 2),
         w_gate,
         w_up,
         w_down,

time: 70.5 us -> 57.6 us (0.82)
  Pallas kernels: 60.4 us -> 53.5 us
  local copies, waits for them, and re-layouts: 8.33 us -> 3.13 us
  other arithmetic: 0.8 us -> 0 us
    pallas_call x1, Pallas kernels: 60.4 us -> 53.5 us  [fused(): pl.pallas_call(functools.partial(fused_kernel, n_expert), out_shape=(jax....]
    unnamed x3 -> x2, local copies, waits for them, and re-layouts: 5.55 us -> 3.13 us
    concatenate x1 -> x0, local copies, waits for them, and re-layouts: 1.53 us -> none  [fused(): jnp.concatenate([moe_rows] + pieces + [jnp.zeros((tokens, spare), jnp.bfl...]
    scatter x1 -> x0, local copies, waits for them, and re-layouts: 1.25 us -> none  [fused(): src_block = jnp.zeros((8, 128), jnp.int32).at[0, :requests].set(move_src)]
    reduce_sum x1 -> x0, other arithmetic: 0.79 us -> none  [fused(): jnp.sum(jnp.where(onehot, expert_weights[:, :, None], 0.0), axis=1)]
where the time goes in v3:
time: 57.6 us; the launch traced here: 57.3 us
  Pallas kernels  53.5 us (93%)
  local copies, waits for them, and re-layouts  3.13 us (5%)
  between operations  0.64 us (1%)
    pallas_call x1, Pallas kernels, fused(): pl.pallas_call(functools.partial(fused_kernel, n_expert), out_shape=(jax....  53.5 us
    unnamed x2, local copies, waits for them, and re-layouts  3.13 us

profile of v3, /device:TPU:0, one launch (start us, length us, event | category | flops | bytes accessed | tf_op | source)
XLA Modules:
  0.0 57.3 jit_solution(11254577062306655079)
XLA Ops:
  0.6 53.5 %shard_map.113 = (bf16[4,7168]{1,0:T(4,128)(2,1)}, bf16[4,64,512]{2,1,0:T(8,128)(2,1)}) custom-call(s32[4]{0:T(128)} %lengths_ref.1, s32[4]{0:T(128)} %own_src_ref.1, s32[4,8]{1,0:T(4,128)} %ids_ref.1, f32[4,8]{1,0:T(4,128)} %weights_ref.1, bf16[4,7168]{1,0:T(4,128)(2,1)} %rows_ref.1, bf16[4,64,576]{2,1,0:T(8,128)(2,1)} %queries_ref.1, ...), custom_call_target="tpu_custom_call" | custom-call | tf_op jit(solution)/shard_map/pallas_call | solution.py:496
  54.2 1.5 %copy.14 = bf16[4,7168]{1,0:T(4,128)(2,1)} copy(bf16[4,7168]{1,0:T(4,128)(2,1)} %get-tuple-element.4) | data formatting | bytes 114688
  55.6 1.7 %copy.15 = bf16[4,64,512]{2,1,0:T(8,128)(2,1)} copy(bf16[4,64,512]{2,1,0:T(8,128)(2,1)} %get-tuple-element.5) | data formatting | bytes 524288

commit v4 on v3

--- a/solution.py
+++ b/solution.py
@@ -86,7 +86,7 @@
 MESH = pl.DeviceIdType.MESH
 CHUNKS = 8
 DEPTH = 4
-DOWN_DEPTH = 3
+DOWN_DEPTH = 4
 LAG = 2
 
 
@@ -307,7 +307,7 @@
             preferred_element_type=jnp.float32,
         )
         hidden = (gate / (1.0 + jnp.exp(-gate)) * up).astype(jnp.bfloat16)
-        hid[e] = (hidden.astype(jnp.float32) * weight).astype(jnp.bfloat16)
+        hid[:, pl.ds(pl.multiple_of(e * ff, 128), ff)] = (hidden.astype(jnp.float32) * weight).astype(jnp.bfloat16)
 
         @pl.when(e + DEPTH < local_experts)
         def _():
@@ -321,15 +321,16 @@
             block(q_all, r2), block(q_all, r2), q_send.at[2], q_recv.at[r2], replica=r1
         )
 
-    half = local_experts // 2
-    lax.fori_loop(0, half, first, 0)
+    early = local_experts // 4
+    late = 5 * local_experts // 8
+    lax.fori_loop(0, early, first, 0)
     q_forward().wait_recv()
     go(q_forward())
     for r in (r1, r3):
         pltpu.make_async_copy(src_all.at[r], src_all.at[r], src_recv.at[r]).wait()
     local_src = pltpu.make_async_copy(src_all, src_smem, src_local)
     local_src.start()
-    lax.fori_loop(half, local_experts, first, 0)
+    lax.fori_loop(early, late, first, 0)
     local_src.wait()
     for r in (r1, r3):
         remote(block(q_all, r), block(q_all, r), q_send.at[0], q_recv.at[r], replica=r1).wait_recv()
@@ -372,6 +373,8 @@
             )
         )
 
+    lax.fori_loop(late, local_experts, first, 0)
+
     def a_copy(c):
         return remote(
             y.at[c, pl.ds(2 * band, 2 * band)], sum_a.at[c], a_send.at[c], a_recv.at[c], replica=r1
@@ -400,14 +403,11 @@
         @pl.when(step < CHUNKS)
         def _():
             down_copy(step).wait()
-            total = jnp.dot(
-                hid[0], down_buf[step % DOWN_DEPTH, 0], preferred_element_type=jnp.float32
+            y[step] = jnp.dot(
+                hid[...],
+                down_buf[step % DOWN_DEPTH].reshape(local_experts * ff, chunk),
+                preferred_element_type=jnp.float32,
             )
-            for e in range(1, local_experts):
-                total += jnp.dot(
-                    hid[e], down_buf[step % DOWN_DEPTH, e], preferred_element_type=jnp.float32
-                )
-            y[step] = total
             a_copy(step).start()
 
             @pl.when(step + DOWN_DEPTH < CHUNKS)
@@ -508,7 +508,7 @@
             pltpu.VMEM((DEPTH, width, ff), bf16),
             pltpu.VMEM((DEPTH, width, ff), bf16),
             pltpu.VMEM((DOWN_DEPTH, local_experts, ff, chunk), bf16),
-            pltpu.VMEM((local_experts, n, ff), bf16),
+            pltpu.VMEM((n, local_experts * ff), bf16),
             pltpu.VMEM((CHUNKS, n, chunk), f32),
             pltpu.VMEM((CHUNKS, 2 * band, chunk), f32),
             pltpu.VMEM((CHUNKS, band, chunk), bf16),

time: 57.6 us -> 56.4 us (0.979)
  Pallas kernels: 53.5 us -> 52.4 us
    pallas_call x1, Pallas kernels: 53.5 us -> 52.4 us  [fused(): pl.pallas_call(functools.partial(fused_kernel, n_expert), out_shape=(jax....]
where the time goes in v4:
time: 56.4 us; the launch traced here: 56.1 us
  Pallas kernels  52.4 us (93%)
  local copies, waits for them, and re-layouts  3.13 us (6%)
  between operations  0.64 us (1%)
    pallas_call x1, Pallas kernels, fused(): pl.pallas_call(functools.partial(fused_kernel, n_expert), out_shape=(jax....  52.4 us
    unnamed x2, local copies, waits for them, and re-layouts  3.13 us

profile of v4, /device:TPU:0, one launch (start us, length us, event | category | flops | bytes accessed | tf_op | source)
XLA Modules:
  0.0 56.1 jit_solution(6770857607807834083)
XLA Ops:
  0.6 52.4 %shard_map.113 = (bf16[4,7168]{1,0:T(4,128)(2,1)}, bf16[4,64,512]{2,1,0:T(8,128)(2,1)}) custom-call(s32[4]{0:T(128)} %lengths_ref.1, s32[4]{0:T(128)} %own_src_ref.1, s32[4,8]{1,0:T(4,128)} %ids_ref.1, f32[4,8]{1,0:T(4,128)} %weights_ref.1, bf16[4,7168]{1,0:T(4,128)(2,1)} %rows_ref.1, bf16[4,64,576]{2,1,0:T(8,128)(2,1)} %queries_ref.1, ...), custom_call_target="tpu_custom_call" | custom-call | tf_op jit(solution)/shard_map/pallas_call | solution.py:496
  53.0 1.5 %copy.14 = bf16[4,7168]{1,0:T(4,128)(2,1)} copy(bf16[4,7168]{1,0:T(4,128)(2,1)} %get-tuple-element.4) | data formatting | bytes 114688
  54.5 1.7 %copy.15 = bf16[4,64,512]{2,1,0:T(8,128)(2,1)} copy(bf16[4,64,512]{2,1,0:T(8,128)(2,1)} %get-tuple-element.5) | data formatting | bytes 524288
